TPU v7x, 256 devices: a whole 4x4x8 slice. The times are simulated.
256 devices in a mesh: head: 4 (over x), outer: 16 (over y, z_lo, core), inner: 4 (over z_hi).
Axes of the slice: x: 4, y: 4, z: 8 (z_hi: 4, z_lo: 2; z = z_hi * 2 + z_lo), core: 2. Of those that a mesh axis runs over, the one named last changes fastest.
Arguments:
- queries: bfloat16 [128, 128, 8192], P(('outer', 'inner'), 'head'), may hold values from -5 to 5
- keys: bfloat16 [128, 128, 1024], P(('outer', 'inner'), 'head'), may hold values from -5 to 5
- values: bfloat16 [128, 128, 1024], P(('outer', 'inner'), 'head'), may hold values from -6 to 6
- half_order: int32 [128], replicated, may hold values from 0 to 127, each once
- window: int32 [8], replicated, may hold values from 4 to 16, as said below
Outputs:
- attended: bfloat16 [128, 128, 8192], P(('outer', 'inner'), 'head')
Inputs may be any that keep to these rules, and one draw needn't show every extreme that they name: `half_order`: a permutation of 0 to 127. Some key head has window 16.
All inputs are finite; a program needn't handle non-finite values.
Results may differ from a plain program's by a relative error of at most 0.0045.
Values may be sent and summed in bfloat16 or wider, within the bound.
A program may use at most 128 MiB of HBM per device.

v0:
```python
import math

import jax
import jax.numpy as jnp
from jax import lax
from jax.sharding import PartitionSpec as P

HD = 128
WIN = 16


def body(queries, keys, values, half_order, window):
    queries_here, keys_here, values_here = (
        lax.all_to_all(queries, "head", split_axis=2, concat_axis=1, tiled=True),
        lax.all_to_all(keys, "head", split_axis=2, concat_axis=1, tiled=True),
        lax.all_to_all(values, "head", split_axis=2, concat_axis=1, tiled=True),
    )
    half_count, half_rows, feature_width = queries_here.shape
    kv_local = keys_here.shape[2] // HD
    group_size = feature_width // HD // kv_local
    cycle_index = lax.axis_index("outer") * lax.axis_size("inner") + lax.axis_index("inner")
    my_blocks = lax.dynamic_slice_in_dim(half_order, cycle_index * half_count, half_count)
    my_window = lax.dynamic_slice_in_dim(window, lax.axis_index("head") * kv_local, kv_local)
    grouped = queries_here.reshape(half_count, half_rows, kv_local, group_size, HD)
    row_index = jnp.arange(half_rows, dtype=jnp.int32)
    score_scale = 1.0 / math.sqrt(HD)
    all_keys, all_values = (
        lax.all_gather(keys_here, ("outer", "inner"), axis=0, tiled=True),
        lax.all_gather(values_here, ("outer", "inner"), axis=0, tiled=True),
    )
    halves_all = all_keys.shape[0]
    inverse = (
        jnp.zeros((halves_all,), jnp.int32)
        .at[half_order]
        .set(jnp.arange(halves_all, dtype=jnp.int32))
    )
    padding = jnp.zeros((WIN, half_rows, all_keys.shape[2]), jnp.bfloat16)
    pad_keys = jnp.concatenate([padding, all_keys[inverse]], 0)
    pad_values = jnp.concatenate([padding, all_values[inverse]], 0)
    slab_rows = jnp.arange(WIN * half_rows, dtype=jnp.int32)
    results = []
    for which_half in range(half_count):
        block = my_blocks[which_half]
        key_slab = lax.dynamic_slice_in_dim(pad_keys, block + 1, WIN, 0).reshape(
            WIN * half_rows, kv_local, HD
        )
        value_slab = lax.dynamic_slice_in_dim(pad_values, block + 1, WIN, 0).reshape(
            WIN * half_rows, kv_local, HD
        )
        key_blocks = block - WIN + 1 + slab_rows // half_rows
        key_pos = key_blocks * half_rows + slab_rows % half_rows
        query_pos = block * half_rows + row_index
        scores = (
            jnp.einsum(
                "tgjd,sgd->gjts", grouped[which_half], key_slab, preferred_element_type=jnp.float32
            )
            * score_scale
        )
        later = (key_pos[None, :] <= query_pos[:, None]) & (key_blocks >= 0)[None, :]
        inside = (block - key_blocks)[None, :] < my_window[:, None]
        seen = later[None, None, :, :] & inside[:, None, None, :]
        masked = jnp.where(seen, scores, -1e30)
        peak = jnp.max(masked, axis=-1, keepdims=True)
        weights = jnp.where(seen, jnp.exp(scores - peak), 0.0)
        denominator = jnp.sum(weights, axis=-1)
        numerator = jnp.einsum(
            "gjts,sgd->tgjd",
            weights.astype(jnp.bfloat16),
            value_slab,
            preferred_element_type=jnp.float32,
        )
        result = numerator / jnp.transpose(denominator, (2, 0, 1))[..., None]
        results.append(result.astype(jnp.bfloat16).reshape(half_rows, feature_width))
    stacked = jnp.stack(results, 0)
    return lax.all_to_all(stacked, "head", split_axis=1, concat_axis=2, tiled=True)


def solution(mesh):
    return jax.shard_map(
        body,
        mesh=mesh,
        in_specs=(
            P(("outer", "inner"), "head", None),
            P(("outer", "inner"), "head", None),
            P(("outer", "inner"), "head", None),
            P(),
            P(),
        ),
        out_specs=P(("outer", "inner"), "head", None),
        check_vma=False,
    )
```

profile of v0, /device:TPU:1, one launch (start us, length us, event | category | flops | bytes accessed | tf_op | source)
XLA Modules:
  0.0 493.8 jit_solution(6117603616719893766)
XLA Ops:
  6.5 1.2 copy.38
  7.7 0.5 reshape.255
  8.3 9.5 %all_to_all.69 = bf16[4,2,8192]{2,1,0:T(2,128)(2,1)S(1)} all-to-all(bf16[4,2,8192]{2,1,0:T(2,128)(2,1)S(1)} %reshape.255), channel_id=1, replica_groups=mesh['head'=4,'outer'=16,'inner'=4] {'head'}, dimensions={0} | all-to-all | bytes 262144 | tf_op jit(solution)/shard_map/all_to_all | solution.py:16
  17.7 0.3 reshape.256
  18.0 0.4 copy.66
  18.4 0.6 copy.40
  19.1 1.2 copy.42
  20.4 0.5 reshape.251
  20.9 7.2 %all_to_all.70 = bf16[4,2,8192]{2,1,0:T(2,128)(2,1)S(1)} all-to-all(bf16[4,2,8192]{2,1,0:T(2,128)(2,1)S(1)} %reshape.251), channel_id=1, replica_groups=mesh['head'=4,'outer'=16,'inner'=4] {'head'}, dimensions={0} | all-to-all | bytes 262144 | tf_op jit(solution)/shard_map/all_to_all | solution.py:15
  28.1 0.3 reshape.252
  28.3 0.4 copy.70
  28.8 0.7 copy.44
  29.4 9.2 %copy.46 = bf16[2,32,8192]{1,0,2:T(2,128)(2,1)} copy(bf16[2,32,8192]{2,1,0:T(8,128)(2,1)} %param.5) | data formatting | bytes 2097152 | tf_op args[0]
  38.6 6.4 %reshape.253 = bf16[4,2,65536]{2,1,0:T(2,128)(2,1)} reshape(bf16[8192,2,32]{2,1,0:T(2,128)(2,1)} %bitcast.82) | data formatting | bytes 2097152
  45.1 3.5 all-to-all-start.2
  48.7 0.6 fusion.90
  54.4 1.2 scatter_custom_fusion
  55.6 0.6 fusion.72
  56.2 0.7 fusion.73
  56.9 0.1 broadcast_compare_fusion.1
  57.0 1.5 compare_and_fusion.1
  58.5 2.1 broadcast_and_fusion.1
  60.5 1.4 compare_and_fusion
  62.0 2.0 broadcast_and_fusion
  64.1 3.5 reshape.254
  67.6 9.0 %copy.47 = bf16[2,32,4,2048]{3,1,2,0:T(8,128)(2,1)S(1)} copy(bf16[2,32,4,2048]{1,0,3,2:T(2,128)(2,1)} %bitcast.81) | data formatting | bytes 2097152 | tf_op jit(solution)/shard_map/all_to_all | solution.py:14
  76.5 0.1 fusion.89
  76.7 0.9 copy.83
  77.5 0.9 copy.84
  78.5 134.5 %all-gather.3.cloned.1.call-done = bf16[128,128,256]{2,1,0:T(8,128)(2,1)} async-done(((bf16[2,128,256]{2,1,0:T(8,128)(2,1)}), bf16[128,128,256]{2,1,0:T(8,128)(2,1)}) %all-gather.3.cloned.1.call-update) | async-done | bytes 8388624 | tf_op jit(solution)/shard_map/all_gather | solution.py:29
  213.0 10.0 %gather_fusion = bf16[128,128,256]{2,1,0:T(8,128)(2,1)} fusion(bf16[128,128,256]{2,1,0:T(8,128)(2,1)} %all-gather.3.cloned.1.call-done, s32[1024]{0:T(1024)S(1)} %pad_clamp_fusion), kind=kCustom, calls=%fused_computation | custom fusion | bytes 16777728 | tf_op jit(solution)/shard_map/gather | solution.py:39
  223.0 187.4 %all-gather.5.cloned.1.call-done = bf16[128,128,256]{2,1,0:T(8,128)(2,1)} async-done(((bf16[2,128,256]{2,1,0:T(8,128)(2,1)}), bf16[128,128,256]{2,1,0:T(8,128)(2,1)}) %all-gather.5.cloned.1.call-update) | async-done | bytes 8388624 | tf_op jit(solution)/shard_map/all_gather | solution.py:28
  410.3 9.9 %gather_fusion.1 = bf16[128,128,256]{2,1,0:T(8,128)(2,1)} fusion(bf16[128,128,256]{2,1,0:T(8,128)(2,1)} %all-gather.5.cloned.1.call-done, s32[1024]{0:T(1024)S(1)} %pad_clamp_fusion), kind=kCustom, calls=%fused_computation.1 | custom fusion | bytes 16777728 | tf_op jit(solution)/shard_map/gather | solution.py:38
  420.3 4.2 pad_dynamic-slice_fusion.1
  424.5 2.2 reshape.246
  426.7 1.1 reshape.245
  427.8 11.4 %fusion.100 = (f32[2,8,128]{2,1,0:T(8,128)S(1)}, bf16[2,8,128,2048]{2,3,1,0:T(8,128)(2,1)}) fusion(pred[2,128,2048]{1,2,0:T(8,128)(4,1)} %broadcast_and_fusion.1, bf16[2048,2,128,1]{2,1,0,3:T(2,128)(2,1)} %bitcast.94, bf16[128,2,8,128]{3,2,1,0:T(8,128)(2,1)} %bitcast.100), kind=kOutput, calls=%fused_computation.93 | convolution fusion | flops 2176845824 | bytes 10493952 | tf_op jit(solution)/shard_map/sub | solution.py:64
  439.2 5.5 %fusion.36 = bf16[128,2,8,128]{0,3,2,1:T(8,128)(2,1)} fusion(bf16[2,8,128,2048]{2,3,1,0:T(8,128)(2,1)} %get-tuple-element.18, bf16[2048,2,128,1]{2,1,0,3:T(2,128)(2,1)S(1)} %bitcast.91, f32[128,2,8]{0,2,1:T(8,128)S(1)} %bitcast.103), kind=kOutput, calls=%fused_computation.37 | convolution fusion | flops 1074266112 | bytes 9969664 | tf_op jit(solution)/shard_map/gjts,sgd->tgjd/dot_general | solution.py:66
  444.8 2.5 copy.56
  447.2 1.1 reshape.248
  448.4 0.3 reshape.247
  448.6 11.3 %fusion.91 = (f32[2,8,128]{2,1,0:T(8,128)S(1)}, bf16[2,8,128,2048]{2,3,1,0:T(8,128)(2,1)}) fusion(pred[2,128,2048]{1,2,0:T(8,128)(4,1)} %broadcast_and_fusion, bf16[2048,2,128,1]{2,1,0,3:T(2,128)(2,1)} %bitcast.92, bf16[128,2,8,128]{3,2,1,0:T(8,128)(2,1)} %bitcast.99), kind=kOutput, calls=%fused_computation.92 | convolution fusion | flops 2176845824 | bytes 10493952 | tf_op jit(solution)/shard_map/sub | solution.py:64
  459.9 5.5 %fusion.39 = bf16[128,2,8,128]{0,3,2,1:T(8,128)(2,1)} fusion(bf16[2,8,128,2048]{2,3,1,0:T(8,128)(2,1)} %get-tuple-element.16, bf16[2048,2,128,1]{2,1,0,3:T(2,128)(2,1)S(1)} %bitcast.93, f32[128,2,8]{0,2,1:T(8,128)S(1)} %bitcast.104), kind=kOutput, calls=%fused_computation.38 | convolution fusion | flops 1074266112 | bytes 9969664 | tf_op jit(solution)/shard_map/gjts,sgd->tgjd/dot_general | solution.py:66
  465.4 2.5 copy.57
  467.9 2.4 pad_maximum_fusion
  470.4 15.2 %all_to_all.71 = bf16[2,128,2048]{2,0,1:T(2,128)(2,1)S(1)} all-to-all(bf16[2,128,2048]{2,0,1:T(2,128)(2,1)S(1)} %pad_maximum_fusion), channel_id=1, replica_groups=mesh['head'=4,'outer'=16,'inner'=4] {'head'}, dimensions={1} | all-to-all | bytes 2097152 | tf_op jit(solution)/shard_map/all_to_all | solution.py:75
  485.5 0.3 copy.58
  485.9 1.0 copy.82
  (21 shorter events, 0.3 us)
Async XLA Ops:
  6.5 206.5 %all-gather.3.cloned.1.call-start = ((), (), s32[]{:S(2)}) async-start(), calls=%async_computation.4 | async-start | bytes 8519680 | tf_op jit(solution)/shard_map/all_gather | solution.py:29
  18.0 30.6 %copy-start.2 = (s32[128]{0:T(128)S(1)}, s32[128]{0:T(128)}, u32[]{:S(2)}) copy-start(s32[128]{0:T(128)} %param.8) | copy-start | bytes 1540
  18.0 36.3 %copy-start.1 = (s32[8]{0:T(128)S(1)}, s32[8]{0:T(128)}, u32[]{:S(2)}) copy-start(s32[8]{0:T(128)} %param.9) | copy-start | bytes 100
  19.1 391.2 %all-gather.5.cloned.1.call-start = ((), (), s32[]{:S(2)}) async-start(), calls=%async_computation.5 | async-start | bytes 8519680 | tf_op jit(solution)/shard_map/all_gather | solution.py:28
  45.1 19.0 %all-to-all-start.2 = ((bf16[4,2,65536]{2,1,0:T(2,128)(2,1)}), bf16[4,2,65536]{2,1,0:T(2,128)(2,1)S(1)}, u32[]{:S(2)}, u32[]{:S(2)}) async-start(bf16[4,2,65536]{2,1,0:T(2,128)(2,1)} %reshape.253), calls=%async_computation.2 | async-start | bytes 2097152 | tf_op jit(solution)/shard_map/all_to_all | solution.py:14
  427.8 11.4 %copy-start = (bf16[2048,2,128]{2,1,0:T(2,128)(2,1)S(1)}, bf16[2048,2,128]{2,1,0:T(2,128)(2,1)}, u32[]{:S(2)}) copy-start(bf16[2048,2,128]{2,1,0:T(2,128)(2,1)} %reshape.245) | copy-start | bytes 3145732
Sparse Core Ops, SparseCore 0:
  19.2 193.7 all-gather.2
  214.8 195.4 all-gather.4
where the time goes:
time: 504 us; the launch traced here: 494 us
  waiting for transfers between devices  322 us (64%)
  local copies, waits for them, and re-layouts  73.2 us (15%)
  matrix products  33.7 us (7%)
  blocking collectives  31.8 us (6%)
  between operations  18.7 us (4%)
  other arithmetic  10.9 us (2%)
    all_gather x1, waiting for transfers between devices, body(): lax.all_gather(keys_here, ('outer', 'inner'), axis=0, tiled=True)  187 us
    all_gather x1, waiting for transfers between devices, body(): lax.all_gather(values_here, ('outer', 'inner'), axis=0, tiled=True)  135 us
    unnamed x17, local copies, waits for them, and re-layouts  24.9 us
    sub x2, matrix products, body(): weights = jnp.where(seen, jnp.exp(scores - peak), 0.0)  22.7 us
    all_to_all x1, blocking collectives, body(): lax.all_to_all(stacked, 'head', split_axis=1, concat_axis=2, tiled=True)  15.2 us
    dot_general x2, matrix products, body(): jnp.einsum('gjts,sgd->tgjd', weights.astype(jnp.bfloat16), value_slab, pr...  11 us
  transfers between devices with their start and end apart: 3, of which 2 were waited for; matrix products, arithmetic and copies ran while one was open for 11% of the time, Pallas kernels for 0%

commit v1 on v0

v1 whole, which is shorter than its diff:
```python
import functools
import math

import jax
import jax.numpy as jnp
import numpy as np
from jax import lax
from jax.experimental import pallas as pl
from jax.experimental.pallas import tpu as pltpu
from jax.sharding import PartitionSpec as P

HD = 128
WIN = 16
ROWS = 128
GROUP = 8
LOG2E = 1.4426950408889634
REL = [(dx, dzl) for dzl in (0, 1) for dx in range(4)]
RING = (0, -1, 1, 2)
MESH = pl.DeviceIdType.MESH


def attend_block(b, idx_ref, vis_ref, qbuf, kv, obuf, kslab, vslab):
    diag = kv[idx_ref[b * WIN + WIN - 1], 0]
    first = jnp.broadcast_to(diag[0:1, :].astype(jnp.float32), (ROWS, HD)).astype(jnp.bfloat16)
    for k in range(WIN):
        slot = idx_ref[b * WIN + k]
        seen_f32 = jnp.full((ROWS, HD), vis_ref[b * WIN + k].astype(jnp.float32))
        seen, unseen = seen_f32.astype(jnp.bfloat16), (1.0 - seen_f32).astype(jnp.bfloat16)
        rows = pl.ds(k * ROWS, ROWS)
        keys = kv[slot, 0] * seen + first * unseen
        kslab[rows, 0:HD] = keys
        kslab[rows, HD : 2 * HD] = keys
        vslab[rows, 0:HD] = kv[slot, 1] * seen
        vslab[rows, HD : 2 * HD] = seen
    row = lax.broadcasted_iota(jnp.int32, (ROWS, ROWS), 0)
    col = lax.broadcasted_iota(jnp.int32, (ROWS, ROWS), 1)
    causal = jnp.concatenate([col <= row] * 2, 0)

    def pair(j, carry):
        lanes = pl.ds(pl.multiple_of(j * 2 * HD, 2 * HD), 2 * HD)
        q = qbuf[b, :, lanes]
        q = jnp.concatenate([q[:, :HD], q[:, HD:]], 0).astype(jnp.float32) * (LOG2E / math.sqrt(HD))
        high = q.astype(jnp.bfloat16)
        low = (q - high.astype(jnp.float32)).astype(jnp.bfloat16)
        s = lax.dot_general(
            jnp.concatenate([high, low], 1), kslab[...], (((1,), (1,)), ((), ())),
            preferred_element_type=jnp.float32,
        )
        edge = (WIN - 1) * ROWS
        s = jnp.concatenate([s[:, :edge], jnp.where(causal, s[:, edge:], -1e30)], 1)
        peak = jnp.max(s, axis=1, keepdims=True)
        p = jnp.exp2(s - peak).astype(jnp.bfloat16)
        o = jnp.dot(p, vslab[...], preferred_element_type=jnp.float32)
        r = (o[:, :HD] / o[:, HD:]).astype(jnp.bfloat16)
        obuf[b, :, lanes] = jnp.concatenate([r[:ROWS], r[ROWS:]], 1)
        return carry

    lax.fori_loop(0, GROUP // 2, pair, 0)


def kernel(idx_ref, vis_ref, q_ref, k_ref, v_ref, o_ref, qbuf, kv, obuf, kslab, vslab,
           a_send, a_recv, g_send, g_recv, o_send, o_recv, local):
    x = lax.axis_index("head")
    outer = lax.axis_index("outer")
    zh = lax.axis_index("inner")
    y, zl, c = outer // 4, (outer // 2) % 2, outer % 2

    def dev(dx=0, dy=0, dzl=0, dc=0, dzh=0):
        yy = (y + dy + 4) % 4
        ll = (zl + dzl) % 2
        cc = (c + dc) % 2
        return {"head": (x + dx + 4) % 4, "outer": yy * 4 + ll * 2 + cc, "inner": (zh + dzh + 4) % 4}

    def slot(dy=0, dzh=0, dc=0):
        return ((((y + dy + 4) % 4) * 4 + (zh + dzh + 4) % 4) * 2 + (c + dc) % 2) * 4

    barrier = pltpu.get_barrier_semaphore()
    partners = [dev(dx=dx, dzl=dzl) for dx, dzl in REL[1:]]
    partners += [dev(dzh=1), dev(dzh=-1), dev(dy=1), dev(dy=-1), dev(dc=1)]
    for partner in partners:
        pl.semaphore_signal(barrier, inc=1, device_id=partner, device_id_type=MESH)
    pl.semaphore_wait(barrier, len(partners))

    sent = []

    def exchange(src, width, dst, send, recv, here):
        arriving = []
        for n, (dx, dzl) in enumerate(REL):
            xx, ll = (x + dx) % 4, (zl + dzl) % 2
            lanes = pl.ds(pl.multiple_of((xx * 2 + ll) * width, width), width)
            if n == 0:
                copy = pltpu.make_async_copy(src.at[:, :, lanes], dst(x, zl), here)
                copy.start()
                arriving.append(copy.wait)
            else:
                copy = pltpu.make_async_remote_copy(
                    src.at[:, :, lanes], dst(x, zl), send.at[n], recv.at[n],
                    device_id=dev(dx=dx, dzl=dzl), device_id_type=MESH)
                copy.start()
                sent.append(copy)
                back = pltpu.make_async_remote_copy(
                    src.at[:, :, lanes], dst((x - dx + 4) % 4, ll), send.at[n], recv.at[n],
                    device_id=dev(dx=dx, dzl=dzl), device_id_type=MESH)
                arriving.append(back.wait_recv)
        return arriving

    own = slot()
    arriving = []
    for which, src in ((0, k_ref), (1, v_ref)):
        arriving += exchange(
            src, HD,
            lambda xx, ll, which=which: kv.at[pl.ds(own + 2 * ll, 2), which, pl.ds(32 * xx, 32), :],
            a_send.at[which], a_recv.at[which], local.at[which])
    queries_in = exchange(
        q_ref, GROUP * HD,
        lambda xx, ll: qbuf.at[pl.ds(2 * ll, 2), pl.ds(32 * xx, 32), :],
        a_send.at[2], a_recv.at[2], local.at[2])
    for wait in arriving:
        wait()

    names = {}

    def copy_of(name, first, count, device):
        n = names.setdefault(name, len(names))
        part = kv.at[pl.ds(first, count)]
        return pltpu.make_async_remote_copy(
            part, part, g_send.at[n], g_recv.at[n], device_id=device, device_id_type=MESH)

    def send(name, first, count, device):
        copy = copy_of(name, first, count, device)
        copy.start()
        sent.append(copy)

    def arrived(name, first, count):
        copy_of(name, first, count, dev(dc=1)).wait_recv()

    pending = []

    def share(name, dy, dzh, half=None):
        off, count = (0, 4) if half is None else (2 * half, 2)
        send(("c", name), slot(dy, dzh) + off, count, dev(dc=1))
        pending.append((("c", name), slot(dy, dzh, 1) + off, count))

    def along_y(r):
        send(("y+", r), slot(0, r), 4, dev(dy=1))
        send(("y-", r), slot(0, r), 4, dev(dy=-1))
        share((0, r), 0, r)

    def onward(r):
        arrived(("y+", r), slot(-1, r), 4)
        send(("yy+", r), slot(-1, r), 2, dev(dy=1))
        share((-1, r), -1, r)
        arrived(("y-", r), slot(1, r), 4)
        send(("yy-", r), slot(1, r) + 2, 2, dev(dy=-1))
        share((1, r), 1, r)

    def opposite(r):
        arrived(("yy+", r), slot(2, r), 2)
        share((2, r, 0), 2, r, 0)
        arrived(("yy-", r), slot(2, r) + 2, 2)
        share((2, r, 1), 2, r, 1)

    send("z+", slot(), 4, dev(dzh=1))
    send("z-", slot(), 4, dev(dzh=-1))
    along_y(0)
    arrived("z+", slot(0, -1), 4)
    send("zz+", slot(0, -1), 2, dev(dzh=1))
    along_y(-1)
    arrived("z-", slot(0, 1), 4)
    send("zz-", slot(0, 1) + 2, 2, dev(dzh=-1))
    along_y(1)
    onward(0)
    arrived("zz+", slot(0, 2), 2)
    arrived("zz-", slot(0, 2) + 2, 2)
    along_y(2)
    onward(-1)
    onward(1)
    opposite(0)
    onward(2)
    opposite(-1)
    opposite(1)
    opposite(2)
    for wait in queries_in:
        wait()
    for item in pending:
        arrived(*item)

    head = x * 2 + zl
    lanes = pl.ds(pl.multiple_of(head * GROUP * HD, GROUP * HD), GROUP * HD)

    def returns(dzl, i, start):
        b = 2 * ((zl + dzl) % 2) + i
        for dx in range(4):
            xx = (x + dx) % 4
            src = obuf.at[b, pl.ds(32 * xx, 32), :]
            if dx == 0 and dzl == 0:
                copy = pltpu.make_async_copy(src, o_ref.at[i, :, lanes], local.at[3 + i])
                copy.start() if start else copy.wait()
                continue
            n = dzl * 4 + dx
            copy = pltpu.make_async_remote_copy(
                src, o_ref.at[i, :, lanes], o_send.at[n, i], o_recv.at[n, i],
                device_id=dev(dx=dx, dzl=dzl), device_id_type=MESH)
            if start:
                copy.start()
            else:
                copy.wait_send()
                from_head = ((x - dx + 4) % 4) * 2 + (zl + dzl) % 2
                there = pl.ds(pl.multiple_of(from_head * GROUP * HD, GROUP * HD), GROUP * HD)
                pltpu.make_async_remote_copy(
                    src, o_ref.at[i, :, there], o_send.at[n, i], o_recv.at[n, i],
                    device_id=dev(dx=dx, dzl=dzl), device_id_type=MESH).wait_recv()

    for dzl in (1, 0):
        for i in range(2):
            b = 2 * ((zl + dzl) % 2) + i
            attend_block(b, idx_ref, vis_ref, qbuf, kv, obuf, kslab, vslab)
            returns(dzl, i, True)
    for copy in sent:
        copy.wait_send()
    for dzl in (1, 0):
        for i in range(2):
            returns(dzl, i, False)


def body(queries, keys, values, half_order, window):
    x = lax.axis_index("head")
    outer = lax.axis_index("outer")
    zh = lax.axis_index("inner")
    y, zl, c = outer // 4, (outer // 2) % 2, outer % 2
    slots = np.arange(128).reshape(4, 4, 2, 2, 2).transpose(0, 3, 2, 1, 4).reshape(128).astype(np.int32)
    place = jnp.sum(jnp.where(half_order[:, None] == jnp.arange(128)[None, :], slots[:, None], 0), 0)
    mine = ((y * 4 + np.repeat(np.arange(2), 2) * 2 + c) * 4 + zh) * 2 + np.tile(np.arange(2), 2)
    wanted = half_order[mine][:, None] + jnp.arange(1 - WIN, 1, dtype=jnp.int32)[None, :]
    back = WIN - 1 - jnp.arange(WIN, dtype=jnp.int32)[None, :]
    vis = ((wanted >= 0) & (back < window[x * 2 + zl])).astype(jnp.int32)
    idx = place[jnp.maximum(wanted, 0)]
    smem = pl.BlockSpec(memory_space=pltpu.SMEM)
    hbm = pl.BlockSpec(memory_space=pl.ANY)
    dma = pltpu.SemaphoreType.DMA
    return pl.pallas_call(
        kernel,
        out_shape=jax.ShapeDtypeStruct(queries.shape, jnp.bfloat16),
        in_specs=[smem, smem, hbm, hbm, hbm],
        out_specs=hbm,
        scratch_shapes=[
            pltpu.VMEM((4, ROWS, GROUP * HD), jnp.bfloat16),
            pltpu.VMEM((128, 2, ROWS, HD), jnp.bfloat16),
            pltpu.VMEM((4, ROWS, GROUP * HD), jnp.bfloat16),
            pltpu.VMEM((WIN * ROWS, 2 * HD), jnp.bfloat16),
            pltpu.VMEM((WIN * ROWS, 2 * HD), jnp.bfloat16),
            dma((3, 8)), dma((3, 8)),
            dma((48,)), dma((48,)),
            dma((8, 2)), dma((8, 2)),
            dma((5,)),
        ],
        compiler_params=pltpu.CompilerParams(
            collective_id=0, has_side_effects=True, vmem_limit_bytes=48 * 1024 * 1024),
    )(idx.reshape(-1), vis.reshape(-1), queries, keys, values)


def solution(mesh):
    rows = P(("outer", "inner"), "head", None)
    return jax.shard_map(
        body,
        mesh=mesh,
        in_specs=(rows, rows, rows, P(), P()),
        out_specs=rows,
        check_vma=False,
    )
```

time: 504 us -> 108 us (0.21); the launches traced: 494 us -> 108 us
  waiting for transfers between devices: 322 us -> 0 us
  Pallas kernels: 0 us -> 102 us
  local copies, waits for them, and re-layouts: 73.2 us -> 4.92 us
  matrix products: 33.7 us -> 0 us
  blocking collectives: 31.8 us -> 0 us
  between operations: 18.7 us -> 0.09 us
  other arithmetic: 10.9 us -> 0.97 us
    all_gather x2 -> x0, waiting for transfers between devices: 322 us -> none  [the longest x1 187 us: body(): lax.all_gather(keys_here, ('outer', 'inner'), axis=0, tiled=True)]
    pallas_call x0 -> x1, Pallas kernels: none -> 102 us  [body(): pl.pallas_call(kernel, out_shape=jax.ShapeDtypeStruct(queries.shape, jnp....]
    all_to_all x3 -> x0, blocking collectives: 31.8 us -> none  [the longest x1 15.2 us: body(): lax.all_to_all(stacked, 'head', split_axis=1, concat_axis=2, tiled=True)]
    sub x2 -> x0, matrix products: 22.7 us -> none  [body(): weights = jnp.where(seen, jnp.exp(scores - peak), 0.0)]
    unnamed x17, local copies, waits for them, and re-layouts: 24.9 us -> 2.75 us
    gather x2, local copies, waits for them, and re-layouts: 19.9 us -> 1.41 us  [the longest x1 0.77 us: body(): idx = place[jnp.maximum(wanted, 0)]]
    all_to_all x7 -> x0, local copies, waits for them, and re-layouts: 12.5 us -> none  [the longest x1 8.97 us: body(): lax.all_to_all(queries, 'head', split_axis=2, concat_axis=1, tiled=True)]
    dot_general x2 -> x0, matrix products: 11 us -> none  [body(): jnp.einsum('gjts,sgd->tgjd', weights.astype(jnp.bfloat16), value_slab, pr...]
  transfers between devices with their start and end apart: 3 -> 0, of which waited for: 2 -> 0; matrix products, arithmetic and copies ran while one was open for 11% -> 0% of each run, Pallas kernels for 0% -> 0%
where the time goes in v1:
time: 108 us
  Pallas kernels  102 us (94%)
  local copies, waits for them, and re-layouts  4.92 us (5%)
    pallas_call x1, Pallas kernels, body(): pl.pallas_call(kernel, out_shape=jax.ShapeDtypeStruct(queries.shape, jnp....  102 us
    unnamed x17, local copies, waits for them, and re-layouts  2.75 us

profile of v1, /device:TPU:1, one launch (start us, length us, event | category | flops | bytes accessed | tf_op | source)
XLA Modules:
  0.0 107.7 jit_solution(4517396009709959400)
XLA Ops:
  0.0 0.0 copy-start.6
  0.0 0.7 copy-done.6
  0.7 0.6 dynamic_slice.3
  1.2 0.0 copy-start.4
  1.2 0.0 copy-start.5
  1.2 0.7 subtract_compare_fusion
  1.9 0.0 copy-done.4
  1.9 0.0 copy-done.5
  2.0 0.0 copy-start.3
  2.0 0.0 copy-start.7
  2.0 0.6 copy-done.3
  2.6 0.0 copy-done.7
  2.6 0.1 select_reduce_fusion
  2.8 0.6 gather_fusion
  3.4 0.1 fusion.1
  3.5 0.1 reshape.73.vis_ref
  3.6 0.1 add_maximum_fusion
  3.6 0.1 reshape.84
  3.7 0.0 copy-start
  3.7 0.0 copy-start.1
  3.7 0.0 copy-start.2
  3.8 0.8 gather_fusion.1
  4.5 0.4 copy-done
  5.0 0.0 copy-done.1
  5.0 0.0 copy-done.2
  5.0 101.7 %shard_map.82 = bf16[2,32,8192]{2,1,0:T(8,128)(2,1)S(1)} custom-call(s32[64]{0:T(128)S(1)} %gather_fusion.1, s32[64]{0:T(128)S(1)} %reshape.73.vis_ref, bf16[2,32,8192]{2,1,0:T(8,128)(2,1)S(1)} %copy-done, bf16[2,32,1024]{2,1,0:T(8,128)(2,1)S(1)} %copy-done.1, bf16[2,32,1024]{2,1,0:T(8,128)(2,1)S(1)} %copy-done.2), custom_call_target="tpu_custom_call" | custom-call | tf_op jit(solution)/shard_map/pallas_call | solution.py:241
  106.8 1.0 copy.10
  (4 shorter events, 0.0 us)
Async XLA Ops:
  0.0 0.7 copy-start.6
  1.2 0.7 copy-start.4
  1.2 0.7 copy-start.5
  2.0 0.7 copy-start.3
  2.0 0.7 copy-start.7
  3.7 1.2 %copy-start = (bf16[2,32,8192]{2,1,0:T(8,128)(2,1)S(1)}, bf16[2,32,8192]{2,1,0:T(8,128)(2,1)}, u32[]{:S(2)}) copy-start(bf16[2,32,8192]{2,1,0:T(8,128)(2,1)} %q_ref.1) | copy-start | bytes 3145732
  3.7 1.2 %copy-start.1 = (bf16[2,32,1024]{2,1,0:T(8,128)(2,1)S(1)}, bf16[2,32,1024]{2,1,0:T(8,128)(2,1)}, u32[]{:S(2)}) copy-start(bf16[2,32,1024]{2,1,0:T(8,128)(2,1)} %k_ref.1) | copy-start | bytes 393220
  3.7 1.2 %copy-start.2 = (bf16[2,32,1024]{2,1,0:T(8,128)(2,1)S(1)}, bf16[2,32,1024]{2,1,0:T(8,128)(2,1)}, u32[]{:S(2)}) copy-start(bf16[2,32,1024]{2,1,0:T(8,128)(2,1)} %v_ref.1) | copy-start | bytes 393220

commit v2 on v1

--- a/solution.py
+++ b/solution.py
@@ -1,9 +1,7 @@
-import functools
 import math
 
 import jax
 import jax.numpy as jnp
-import numpy as np
 from jax import lax
 from jax.experimental import pallas as pl
 from jax.experimental.pallas import tpu as pltpu
@@ -19,12 +17,16 @@
 MESH = pl.DeviceIdType.MESH
 
 
-def attend_block(b, idx_ref, vis_ref, qbuf, kv, obuf, kslab, vslab):
-    diag = kv[idx_ref[b * WIN + WIN - 1], 0]
+def slot_at(table, n):
+    return jnp.clip(table[0, n], 0, 127)
+
+
+def attend_block(b, table, qbuf, kv, obuf, kslab, vslab):
+    diag = kv[slot_at(table, b * WIN + WIN - 1), 0]
     first = jnp.broadcast_to(diag[0:1, :].astype(jnp.float32), (ROWS, HD)).astype(jnp.bfloat16)
     for k in range(WIN):
-        slot = idx_ref[b * WIN + k]
-        seen_f32 = jnp.full((ROWS, HD), vis_ref[b * WIN + k].astype(jnp.float32))
+        slot = slot_at(table, b * WIN + k)
+        seen_f32 = jnp.full((ROWS, HD), table[1, b * WIN + k].astype(jnp.float32))
         seen, unseen = seen_f32.astype(jnp.bfloat16), (1.0 - seen_f32).astype(jnp.bfloat16)
         rows = pl.ds(k * ROWS, ROWS)
         keys = kv[slot, 0] * seen + first * unseen
@@ -36,8 +38,8 @@
     col = lax.broadcasted_iota(jnp.int32, (ROWS, ROWS), 1)
     causal = jnp.concatenate([col <= row] * 2, 0)
 
-    def pair(j, carry):
-        lanes = pl.ds(pl.multiple_of(j * 2 * HD, 2 * HD), 2 * HD)
+    for j in range(GROUP // 2):
+        lanes = slice(j * 2 * HD, (j + 1) * 2 * HD)
         q = qbuf[b, :, lanes]
         q = jnp.concatenate([q[:, :HD], q[:, HD:]], 0).astype(jnp.float32) * (LOG2E / math.sqrt(HD))
         high = q.astype(jnp.bfloat16)
@@ -53,12 +55,9 @@
         o = jnp.dot(p, vslab[...], preferred_element_type=jnp.float32)
         r = (o[:, :HD] / o[:, HD:]).astype(jnp.bfloat16)
         obuf[b, :, lanes] = jnp.concatenate([r[:ROWS], r[ROWS:]], 1)
-        return carry
-
-    lax.fori_loop(0, GROUP // 2, pair, 0)
-
-
-def kernel(idx_ref, vis_ref, q_ref, k_ref, v_ref, o_ref, qbuf, kv, obuf, kslab, vslab,
+
+
+def kernel(order_ref, window_ref, row_ref, q_ref, k_ref, v_ref, o_ref, qbuf, kv, obuf, kslab, vslab, lookup, table,
            a_send, a_recv, g_send, g_recv, o_send, o_recv, local):
     x = lax.axis_index("head")
     outer = lax.axis_index("outer")
@@ -111,10 +110,21 @@
             src, HD,
             lambda xx, ll, which=which: kv.at[pl.ds(own + 2 * ll, 2), which, pl.ds(32 * xx, 32), :],
             a_send.at[which], a_recv.at[which], local.at[which])
-    queries_in = exchange(
-        q_ref, GROUP * HD,
-        lambda xx, ll: qbuf.at[pl.ds(2 * ll, 2), pl.ds(32 * xx, 32), :],
-        a_send.at[2], a_recv.at[2], local.at[2])
+    lane = lax.broadcasted_iota(jnp.int32, (1, ROWS), 1)
+    block = jnp.zeros((1, ROWS), jnp.int32)
+    for b in range(4):
+        stored = ((y * 4 + b // 2 * 2 + c) * 4 + zh) * 2 + b % 2
+        block = jnp.where(lane // WIN == b, order_ref[stored], block)
+    back = WIN - 1 - lane % WIN
+    wanted = block - back
+    j = lax.broadcasted_iota(jnp.int32, (ROWS, ROWS), 0)
+    slots = (((j // 32) * 4 + (j // 2) % 4) * 2 + (j // 8) % 2) * 4 + (j // 16) % 2 * 2 + j % 2
+    order = jnp.broadcast_to(row_ref[...], (ROWS, ROWS)).T
+    lookup[0:1, :] = jnp.sum(jnp.where(order == wanted, slots, 0), axis=0, keepdims=True)
+    lookup[1:2, :] = ((wanted >= 0) & (back < window_ref[x * 2 + zl])).astype(jnp.int32)
+    lookup[2:8, :] = jnp.zeros((6, ROWS), jnp.int32)
+    listing = pltpu.make_async_copy(lookup, table, local.at[5])
+    listing.start()
     for wait in arriving:
         wait()
 
@@ -141,45 +151,82 @@
         send(("c", name), slot(dy, dzh) + off, count, dev(dc=1))
         pending.append((("c", name), slot(dy, dzh, 1) + off, count))
 
-    def along_y(r):
-        send(("y+", r), slot(0, r), 4, dev(dy=1))
-        send(("y-", r), slot(0, r), 4, dev(dy=-1))
-        share((0, r), 0, r)
-
-    def onward(r):
-        arrived(("y+", r), slot(-1, r), 4)
-        send(("yy+", r), slot(-1, r), 2, dev(dy=1))
+    def along_y(r, h):
+        send(("y+", r, h), slot(0, r) + 2 * h, 2, dev(dy=1))
+        send(("y-", r, h), slot(0, r) + 2 * h, 2, dev(dy=-1))
+
+    def from_y(r, h, down):
+        dy = 1 if down else -1
+        arrived(("y-" if down else "y+", r, h), slot(dy, r) + 2 * h, 2)
+        if down == (h == 1):
+            send(("yy", r, down), slot(dy, r) + 2 * h, 2, dev(dy=-dy))
+
+    def opposite(r):
+        arrived(("yy", r, False), slot(2, r), 2)
+        share((2, r, 0), 2, r, 0)
+        arrived(("yy", r, True), slot(2, r) + 2, 2)
+        share((2, r, 1), 2, r, 1)
+
+    def z(h, down):
+        send(("z", down, h), slot() + 2 * h, 2, dev(dzh=-1 if down else 1))
+
+    def from_z(h, down):
+        r = 1 if down else -1
+        arrived(("z", down, h), slot(0, r) + 2 * h, 2)
+        if down == (h == 1):
+            send(("zz", down), slot(0, r) + 2 * h, 2, dev(dzh=-r))
+
+    z(0, False)
+    z(1, True)
+    along_y(0, 0)
+    along_y(0, 1)
+    z(1, False)
+    z(0, True)
+    share((0, 0), 0, 0)
+    from_z(0, False)
+    along_y(-1, 0)
+    from_z(1, True)
+    along_y(1, 1)
+    from_y(0, 0, False)
+    from_y(0, 1, True)
+    from_z(1, False)
+    along_y(-1, 1)
+    from_z(0, True)
+    along_y(1, 0)
+    share((0, -1), 0, -1)
+    share((0, 1), 0, 1)
+    queries_in = exchange(
+        q_ref, GROUP * HD,
+        lambda xx, ll: qbuf.at[pl.ds(2 * ll, 2), pl.ds(32 * xx, 32), :],
+        a_send.at[2], a_recv.at[2], local.at[2])
+    from_y(0, 1, False)
+    share((-1, 0), -1, 0)
+    from_y(0, 0, True)
+    share((1, 0), 1, 0)
+    arrived(("zz", False), slot(0, 2), 2)
+    along_y(2, 0)
+    arrived(("zz", True), slot(0, 2) + 2, 2)
+    along_y(2, 1)
+    share((0, 2), 0, 2)
+    for r in (-1, 1):
+        from_y(r, 0, False)
+        from_y(r, 1, True)
+    opposite(0)
+    for r in (-1, 1):
+        from_y(r, 1, False)
         share((-1, r), -1, r)
-        arrived(("y-", r), slot(1, r), 4)
-        send(("yy-", r), slot(1, r) + 2, 2, dev(dy=-1))
+        from_y(r, 0, True)
         share((1, r), 1, r)
-
-    def opposite(r):
-        arrived(("yy+", r), slot(2, r), 2)
-        share((2, r, 0), 2, r, 0)
-        arrived(("yy-", r), slot(2, r) + 2, 2)
-        share((2, r, 1), 2, r, 1)
-
-    send("z+", slot(), 4, dev(dzh=1))
-    send("z-", slot(), 4, dev(dzh=-1))
-    along_y(0)
-    arrived("z+", slot(0, -1), 4)
-    send("zz+", slot(0, -1), 2, dev(dzh=1))
-    along_y(-1)
-    arrived("z-", slot(0, 1), 4)
-    send("zz-", slot(0, 1) + 2, 2, dev(dzh=-1))
-    along_y(1)
-    onward(0)
-    arrived("zz+", slot(0, 2), 2)
-    arrived("zz-", slot(0, 2) + 2, 2)
-    along_y(2)
-    onward(-1)
-    onward(1)
-    opposite(0)
-    onward(2)
+    from_y(2, 0, False)
+    from_y(2, 1, True)
     opposite(-1)
     opposite(1)
+    from_y(2, 1, False)
+    share((-1, 2), -1, 2)
+    from_y(2, 0, True)
+    share((1, 2), 1, 2)
     opposite(2)
+    listing.wait()
     for wait in queries_in:
         wait()
     for item in pending:
@@ -214,7 +261,7 @@
     for dzl in (1, 0):
         for i in range(2):
             b = 2 * ((zl + dzl) % 2) + i
-            attend_block(b, idx_ref, vis_ref, qbuf, kv, obuf, kslab, vslab)
+            attend_block(b, table, qbuf, kv, obuf, kslab, vslab)
             returns(dzl, i, True)
     for copy in sent:
         copy.wait_send()
@@ -224,24 +271,13 @@
 
 
 def body(queries, keys, values, half_order, window):
-    x = lax.axis_index("head")
-    outer = lax.axis_index("outer")
-    zh = lax.axis_index("inner")
-    y, zl, c = outer // 4, (outer // 2) % 2, outer % 2
-    slots = np.arange(128).reshape(4, 4, 2, 2, 2).transpose(0, 3, 2, 1, 4).reshape(128).astype(np.int32)
-    place = jnp.sum(jnp.where(half_order[:, None] == jnp.arange(128)[None, :], slots[:, None], 0), 0)
-    mine = ((y * 4 + np.repeat(np.arange(2), 2) * 2 + c) * 4 + zh) * 2 + np.tile(np.arange(2), 2)
-    wanted = half_order[mine][:, None] + jnp.arange(1 - WIN, 1, dtype=jnp.int32)[None, :]
-    back = WIN - 1 - jnp.arange(WIN, dtype=jnp.int32)[None, :]
-    vis = ((wanted >= 0) & (back < window[x * 2 + zl])).astype(jnp.int32)
-    idx = place[jnp.maximum(wanted, 0)]
     smem = pl.BlockSpec(memory_space=pltpu.SMEM)
     hbm = pl.BlockSpec(memory_space=pl.ANY)
     dma = pltpu.SemaphoreType.DMA
     return pl.pallas_call(
         kernel,
         out_shape=jax.ShapeDtypeStruct(queries.shape, jnp.bfloat16),
-        in_specs=[smem, smem, hbm, hbm, hbm],
+        in_specs=[smem, smem, pl.BlockSpec(memory_space=pltpu.VMEM), hbm, hbm, hbm],
         out_specs=hbm,
         scratch_shapes=[
             pltpu.VMEM((4, ROWS, GROUP * HD), jnp.bfloat16),
@@ -249,14 +285,16 @@
             pltpu.VMEM((4, ROWS, GROUP * HD), jnp.bfloat16),
             pltpu.VMEM((WIN * ROWS, 2 * HD), jnp.bfloat16),
             pltpu.VMEM((WIN * ROWS, 2 * HD), jnp.bfloat16),
+            pltpu.VMEM((8, ROWS), jnp.int32),
+            pltpu.SMEM((8, ROWS), jnp.int32),
             dma((3, 8)), dma((3, 8)),
-            dma((48,)), dma((48,)),
+            dma((80,)), dma((80,)),
             dma((8, 2)), dma((8, 2)),
-            dma((5,)),
+            dma((6,)),
         ],
         compiler_params=pltpu.CompilerParams(
             collective_id=0, has_side_effects=True, vmem_limit_bytes=48 * 1024 * 1024),
-    )(idx.reshape(-1), vis.reshape(-1), queries, keys, values)
+    )(half_order, window, half_order.reshape(1, ROWS), queries, keys, values)
 
 
 def solution(mesh):

time: 108 us -> 81.4 us (0.75)
  Pallas kernels: 102 us -> 76.5 us
    pallas_call x1, Pallas kernels: 102 us -> 76.5 us  [body(): pl.pallas_call(kernel, out_shape=jax.ShapeDtypeStruct(queries.shape, jnp....]
    unnamed x17 -> x11, local copies, waits for them, and re-layouts: 2.75 us -> 4.67 us
    gather x2 -> x0, local copies, waits for them, and re-layouts: 1.41 us -> none  [the longest x1 0.77 us: body(): idx = place[jnp.maximum(wanted, 0)]]
where the time goes in v2:
time: 81.4 us; the launch traced here: 81.2 us
  Pallas kernels  76.5 us (94%)
  local copies, waits for them, and re-layouts  4.67 us (6%)
    pallas_call x1, Pallas kernels, body(): pl.pallas_call(kernel, out_shape=jax.ShapeDtypeStruct(queries.shape, jnp....  76.5 us
    unnamed x11, local copies, waits for them, and re-layouts  4.67 us

profile of v2, /device:TPU:1, one launch (start us, length us, event | category | flops | bytes accessed | tf_op | source)
XLA Modules:
  0.0 81.2 jit_solution(9943899996040003489)
XLA Ops:
  0.0 0.0 copy-start.3
  0.0 0.0 copy-start.4
  0.0 0.7 copy-done.3
  0.7 0.0 copy-done.4
  0.7 0.0 copy-start
  0.7 1.2 %copy-done = bf16[2,32,8192]{2,1,0:T(8,128)(2,1)S(1)} copy-done((bf16[2,32,8192]{2,1,0:T(8,128)(2,1)S(1)}, bf16[2,32,8192]{2,1,0:T(8,128)(2,1)}, u32[]{:S(2)}) %copy-start) | copy-done | bytes 1048600
  1.9 0.0 copy-start.1
  1.9 0.9 %copy-done.1 = bf16[2,32,1024]{2,1,0:T(8,128)(2,1)S(1)} copy-done((bf16[2,32,1024]{2,1,0:T(8,128)(2,1)S(1)}, bf16[2,32,1024]{2,1,0:T(8,128)(2,1)}, u32[]{:S(2)}) %copy-start.1) | copy-done | bytes 131096
  2.8 0.0 copy-start.2
  2.8 0.9 %copy-done.2 = bf16[2,32,1024]{2,1,0:T(8,128)(2,1)S(1)} copy-done((bf16[2,32,1024]{2,1,0:T(8,128)(2,1)S(1)}, bf16[2,32,1024]{2,1,0:T(8,128)(2,1)}, u32[]{:S(2)}) %copy-start.2) | copy-done | bytes 131096
  3.7 76.5 %shard_map.55 = bf16[2,32,8192]{2,1,0:T(8,128)(2,1)S(1)} custom-call(s32[128]{0:T(128)S(1)} %copy-done.3, s32[8]{0:T(128)S(1)} %copy-done.4, s32[1,128]{1,0:T(1,128)S(1)} %bitcast.1, bf16[2,32,8192]{2,1,0:T(8,128)(2,1)S(1)} %copy-done, bf16[2,32,1024]{2,1,0:T(8,128)(2,1)S(1)} %copy-done.1, bf16[2,32,1024]{2,1,0:T(8,128)(2,1)S(1)} %copy-done.2), custom_call_target="tpu_custom_call" | custom-call | tf_op jit(solution)/shard_map/pallas_call | solution.py:277
  80.2 1.0 %copy.7 = bf16[2,32,8192]{2,1,0:T(8,128)(2,1)} copy(bf16[2,32,8192]{2,1,0:T(8,128)(2,1)S(1)} %shard_map.55) | data formatting | bytes 2097152
Async XLA Ops:
  0.0 0.7 copy-start.3
  0.0 0.7 copy-start.4
  0.7 1.2 %copy-start = (bf16[2,32,8192]{2,1,0:T(8,128)(2,1)S(1)}, bf16[2,32,8192]{2,1,0:T(8,128)(2,1)}, u32[]{:S(2)}) copy-start(bf16[2,32,8192]{2,1,0:T(8,128)(2,1)} %q_ref.1) | copy-start | bytes 3145732
  1.9 0.9 %copy-start.1 = (bf16[2,32,1024]{2,1,0:T(8,128)(2,1)S(1)}, bf16[2,32,1024]{2,1,0:T(8,128)(2,1)}, u32[]{:S(2)}) copy-start(bf16[2,32,1024]{2,1,0:T(8,128)(2,1)} %k_ref.1) | copy-start | bytes 393220
  2.8 0.9 %copy-start.2 = (bf16[2,32,1024]{2,1,0:T(8,128)(2,1)S(1)}, bf16[2,32,1024]{2,1,0:T(8,128)(2,1)}, u32[]{:S(2)}) copy-start(bf16[2,32,1024]{2,1,0:T(8,128)(2,1)} %v_ref.1) | copy-start | bytes 393220

commit v3 on v2

v3 whole, which is shorter than its diff:
```python
import math

import jax
import jax.numpy as jnp
from jax import lax
from jax.experimental import pallas as pl
from jax.experimental.pallas import tpu as pltpu
from jax.sharding import PartitionSpec as P

HD = 128
WIN = 16
ROWS = 128
GROUP = 8
LOG2E = 1.4426950408889634
TILE = 2
VTILE = 2
REL = [(dx, dzl) for dzl in (0, 1) for dx in range(4)]
RING = (0, -1, 1, 2)
MESH = pl.DeviceIdType.MESH


def slot_at(table, n):
    return jnp.clip(table[0, n], 0, 127)


def key_slab(b, table, kbuf, kslab):
    first = kbuf[slot_at(table, b * WIN + WIN - 1)][0:1, :].astype(jnp.float32)
    first = jnp.broadcast_to(first, (ROWS, HD)).astype(jnp.bfloat16)
    for k in range(WIN):
        seen = jnp.full((ROWS, HD), table[1, b * WIN + k].astype(jnp.float32))
        unseen = (1.0 - seen).astype(jnp.bfloat16)
        keys = kbuf[slot_at(table, b * WIN + k)] * seen.astype(jnp.bfloat16) + first * unseen
        kslab[k * ROWS : (k + 1) * ROWS, 0:HD] = keys
        kslab[k * ROWS : (k + 1) * ROWS, HD : 2 * HD] = keys


def value_slab(b, table, vbuf, vslab):
    for k in range(WIN):
        seen = jnp.full((ROWS, HD), table[1, b * WIN + k].astype(jnp.float32)).astype(jnp.bfloat16)
        vslab[k * ROWS : (k + 1) * ROWS, 0:HD] = vbuf[slot_at(table, b * WIN + k)] * seen
        vslab[k * ROWS : (k + 1) * ROWS, HD : 2 * HD] = seen


def scores(b, j, qbuf, kslab, weights):
    row = lax.broadcasted_iota(jnp.int32, (ROWS, ROWS), 0)
    col = lax.broadcasted_iota(jnp.int32, (ROWS, ROWS), 1)
    causal = jnp.concatenate([col <= row] * TILE, 0)
    for t in range(GROUP // 2 // TILE):
        first = (j * (GROUP // 2) + t * TILE) * HD
        q = qbuf[b, :, first : first + TILE * HD]
        q = jnp.concatenate([q[:, i * HD : (i + 1) * HD] for i in range(TILE)], 0)
        q = q.astype(jnp.float32) * (LOG2E / math.sqrt(HD))
        high = q.astype(jnp.bfloat16)
        low = (q - high.astype(jnp.float32)).astype(jnp.bfloat16)
        s = lax.dot_general(
            jnp.concatenate([high, low], 1), kslab[...], (((1,), (1,)), ((), ())),
            preferred_element_type=jnp.float32,
        )
        edge = (WIN - 1) * ROWS
        s = jnp.concatenate([s[:, :edge], jnp.where(causal, s[:, edge:], -1e30)], 1)
        peak = jnp.max(s, axis=1, keepdims=True)
        weights[t * TILE * ROWS : (t + 1) * TILE * ROWS, :] = jnp.exp2(s - peak).astype(jnp.bfloat16)


def sums(b, j, weights, vslab, obuf):
    for t in range(GROUP // 2 // VTILE):
        o = jnp.dot(weights[t * VTILE * ROWS : (t + 1) * VTILE * ROWS, :], vslab[...], preferred_element_type=jnp.float32)
        r = (o[:, :HD] / o[:, HD:]).astype(jnp.bfloat16)
        for i in range(VTILE):
            first = (j * (GROUP // 2) + t * VTILE + i) * HD
            obuf[b, :, first : first + HD] = r[i * ROWS : (i + 1) * ROWS]


def kernel(order_hbm, window_hbm, row_hbm, q_ref, k_ref, v_ref, o_ref, qbuf, kbuf, vbuf, obuf, weights0, weights1, kslab, vslab, lookup, table, order_ref, window_ref, row_ref,
           a_send, a_recv, g_send, g_recv, o_send, o_recv, local):
    x = lax.axis_index("head")
    outer = lax.axis_index("outer")
    zh = lax.axis_index("inner")
    y, zl, c = outer // 4, (outer // 2) % 2, outer % 2

    def dev(dx=0, dy=0, dzl=0, dc=0, dzh=0):
        yy = (y + dy + 4) % 4
        ll = (zl + dzl) % 2
        cc = (c + dc) % 2
        return {"head": (x + dx + 4) % 4, "outer": yy * 4 + ll * 2 + cc, "inner": (zh + dzh + 4) % 4}

    def slot(dy=0, dzh=0, dc=0):
        return ((((y + dy + 4) % 4) * 4 + (zh + dzh + 4) % 4) * 2 + (c + dc) % 2) * 4

    small = [pltpu.make_async_copy(src, dst, local.at[6 + n]) for n, (src, dst) in enumerate(
        ((order_hbm, order_ref), (window_hbm, window_ref), (row_hbm, row_ref)))]
    for copy in small:
        copy.start()
    barrier = pltpu.get_barrier_semaphore()
    partners = [dev(dx=dx, dzl=dzl) for dx, dzl in REL[1:]]
    partners += [dev(dzh=1), dev(dzh=-1), dev(dy=1), dev(dy=-1), dev(dc=1)]
    for partner in partners:
        pl.semaphore_signal(barrier, inc=1, device_id=partner, device_id_type=MESH)
    pl.semaphore_wait(barrier, len(partners))

    sent = []

    def exchange(src, width, dst, send, recv, here):
        arriving = []
        for n, (dx, dzl) in enumerate(REL):
            xx, ll = (x + dx) % 4, (zl + dzl) % 2
            lanes = pl.ds(pl.multiple_of((xx * 2 + ll) * width, width), width)
            if n == 0:
                copy = pltpu.make_async_copy(src.at[:, :, lanes], dst(x, zl, dzl), here)
                copy.start()
                arriving.append(copy.wait)
            else:
                copy = pltpu.make_async_remote_copy(
                    src.at[:, :, lanes], dst(x, zl, dzl), send.at[n], recv.at[n],
                    device_id=dev(dx=dx, dzl=dzl), device_id_type=MESH)
                copy.start()
                sent.append(copy)
                back = pltpu.make_async_remote_copy(
                    src.at[:, :, lanes], dst((x - dx + 4) % 4, ll, dzl), send.at[n], recv.at[n],
                    device_id=dev(dx=dx, dzl=dzl), device_id_type=MESH)
                arriving.append(back.wait_recv)
        return arriving

    own = slot()
    arriving = []
    bufs = (kbuf, vbuf)
    for which, src, buf in ((0, k_ref, kbuf), (1, v_ref, vbuf)):
        arriving += exchange(
            src, HD,
            lambda xx, ll, dzl, buf=buf: buf.at[pl.ds(own + 2 * ll, 2), pl.ds(32 * xx, 32), :],
            a_send.at[which], a_recv.at[which], local.at[which])
    for copy in small:
        copy.wait()
    lane = lax.broadcasted_iota(jnp.int32, (1, ROWS), 1)
    block = jnp.zeros((1, ROWS), jnp.int32)
    for b in range(4):
        stored = ((y * 4 + (zl + b // 2) % 2 * 2 + c) * 4 + zh) * 2 + b % 2
        block = jnp.where(lane // WIN == b, order_ref[stored], block)
    back = WIN - 1 - lane % WIN
    wanted = block - back
    j = lax.broadcasted_iota(jnp.int32, (ROWS, ROWS), 0)
    slots = (((j // 32) * 4 + (j // 2) % 4) * 2 + (j // 8) % 2) * 4 + (j // 16) % 2 * 2 + j % 2
    order = jnp.broadcast_to(row_ref[...], (ROWS, ROWS)).T
    lookup[0:1, :] = jnp.sum(jnp.where(order == wanted, slots, 0), axis=0, keepdims=True)
    lookup[1:2, :] = ((wanted >= 0) & (back < window_ref[x * 2 + zl])).astype(jnp.int32)
    lookup[2:8, :] = jnp.zeros((6, ROWS), jnp.int32)
    listing = pltpu.make_async_copy(lookup, table, local.at[5])
    listing.start()
    for wait in arriving[:8]:
        wait()

    names = {}

    def copy_of(name, w, first, count, device):
        n = names.setdefault((name, w), len(names))
        part = bufs[w].at[pl.ds(first, count)]
        return pltpu.make_async_remote_copy(
            part, part, g_send.at[n], g_recv.at[n], device_id=device, device_id_type=MESH)

    def send(name, w, first, count, device):
        copy = copy_of(name, w, first, count, device)
        copy.start()
        sent.append(copy)

    def arrived(name, w, first, count):
        copy_of(name, w, first, count, dev(dc=1)).wait_recv()

    pending = ([], [])

    def share(w, dy, dzh, half=None):
        off, count = (0, 4) if half is None else (2 * half, 2)
        name = ("c", dy, dzh, half)
        send(name, w, slot(dy, dzh) + off, count, dev(dc=1))
        pending[w].append((name, w, slot(dy, dzh, 1) + off, count))

    def to_z(w):
        send("z+", w, slot(), 4, dev(dzh=1))
        send("z-", w, slot(), 4, dev(dzh=-1))

    def from_z(w, r):
        arrived("z+" if r < 0 else "z-", w, slot(0, r), 4)
        half = 0 if r < 0 else 2
        send(("zz", r), w, slot(0, r) + half, 2, dev(dzh=-r))

    def from_zz(w):
        arrived(("zz", -1), w, slot(0, 2), 2)
        arrived(("zz", 1), w, slot(0, 2) + 2, 2)

    def to_y(w, r):
        send(("y+", r), w, slot(0, r), 4, dev(dy=1))
        send(("y-", r), w, slot(0, r), 4, dev(dy=-1))

    def from_y(w, r):
        arrived(("y+", r), w, slot(-1, r), 4)
        send(("yy+", r), w, slot(-1, r), 2, dev(dy=1))
        arrived(("y-", r), w, slot(1, r), 4)
        send(("yy-", r), w, slot(1, r) + 2, 2, dev(dy=-1))

    def share_y(w, r):
        share(w, -1, r)
        share(w, 1, r)

    def opposite(w, r):
        arrived(("yy+", r), w, slot(2, r), 2)
        share(w, 2, r, 0)
        arrived(("yy-", r), w, slot(2, r) + 2, 2)
        share(w, 2, r, 1)

    K, V = 0, 1
    to_z(K)
    to_y(K, 0)
    for wait in arriving[8:]:
        wait()
    to_z(V)
    to_y(V, 0)
    share(K, 0, 0)
    share(V, 0, 0)
    from_y(K, 0)
    from_z(K, -1)
    to_y(K, -1)
    from_z(K, 1)
    to_y(K, 1)
    from_y(V, 0)
    share(K, 0, -1)
    share(K, 0, 1)
    share_y(K, 0)
    from_z(V, -1)
    to_y(V, -1)
    from_z(V, 1)
    to_y(V, 1)
    from_zz(K)
    to_y(K, 2)
    queries_in = exchange(
        q_ref, GROUP * HD,
        lambda xx, ll, dzl: qbuf.at[pl.ds(2 * dzl, 2), pl.ds(32 * xx, 32), :],
        a_send.at[2], a_recv.at[2], local.at[2])
    from_y(K, -1)
    from_y(K, 1)
    share(K, 0, 2)
    share_y(K, -1)
    share_y(K, 1)
    from_zz(V)
    to_y(V, 2)
    opposite(K, 0)
    from_y(K, 2)
    share_y(K, 2)
    for r in (-1, 1, 2):
        share(V, 0, r)
    share_y(V, 0)
    from_y(V, -1)
    from_y(V, 1)
    for r in (-1, 1, 2):
        opposite(K, r)
    from_y(V, 2)
    share_y(V, -1)
    share_y(V, 1)
    opposite(V, 0)
    share_y(V, 2)
    opposite(V, -1)
    opposite(V, 1)
    opposite(V, 2)
    listing.wait()
    for wait in queries_in:
        wait()
    for item in pending[K]:
        arrived(*item)
    width = GROUP * HD // 2

    def returns(b, j, start):
        dzl, i = b // 2, b % 2
        part = slice(j * width, (j + 1) * width)

        def copy_to(dx, xx, ll):
            lanes = pl.ds(pl.multiple_of((xx * 2 + ll) * 2 * width + j * width, width), width)
            return pltpu.make_async_remote_copy(
                obuf.at[b, pl.ds(32 * ((x + dx) % 4), 32), part], o_ref.at[i, :, lanes],
                o_send.at[b, dx, j], o_recv.at[b, dx, j], device_id=dev(dx=dx, dzl=dzl), device_id_type=MESH)

        def remote(dx):
            if start:
                copy_to(dx, x, zl).start()
            else:
                copy_to(dx, x, zl).wait_send()
                copy_to(dx, (x - dx + 4) % 4, (zl + dzl) % 2).wait_recv()

        def here():
            lanes = pl.ds(pl.multiple_of((x * 2 + zl) * 2 * width + j * width, width), width)
            copy = pltpu.make_async_copy(
                obuf.at[b, pl.ds(32 * x, 32), part], o_ref.at[i, :, lanes], local.at[9 + 2 * i + j])
            copy.start() if start else copy.wait()

        for dx in (2, 1, 3):
            remote(dx)
        pl.when(dzl == 1)(lambda: remote(0))
        pl.when(dzl == 0)(here)

    def attend(n, last):
        b, after = (n + 2) % 4, (n + 3) % 4
        value_slab(b, table, vbuf, vslab)
        sums(b, 0, weights0, vslab, obuf)
        scores(b, 1, qbuf, kslab, weights1)
        returns(b, 0, True)
        sums(b, 1, weights1, vslab, obuf)
        if not last:
            key_slab(after, table, kbuf, kslab)
            scores(after, 0, qbuf, kslab, weights0)
        returns(b, 1, True)

    def attend_step(n, carry):
        attend(n, False)
        return carry

    def return_step(n, carry):
        returns((n + 2) % 4, 0, False)
        returns((n + 2) % 4, 1, False)
        return carry

    key_slab(2, table, kbuf, kslab)
    scores(2, 0, qbuf, kslab, weights0)
    for item in pending[V]:
        arrived(*item)
    lax.fori_loop(0, 3, attend_step, 0)
    attend(jnp.int32(3), True)
    for copy in sent:
        copy.wait_send()
    lax.fori_loop(0, 4, return_step, 0)


def body(queries, keys, values, half_order, window):
    hbm = pl.BlockSpec(memory_space=pltpu.HBM)
    dma = pltpu.SemaphoreType.DMA
    return pl.pallas_call(
        kernel,
        out_shape=jax.ShapeDtypeStruct(queries.shape, jnp.bfloat16),
        in_specs=[hbm] * 6,
        out_specs=hbm,
        scratch_shapes=[
            pltpu.VMEM((4, ROWS, GROUP * HD), jnp.bfloat16),
            pltpu.VMEM((128, ROWS, HD), jnp.bfloat16),
            pltpu.VMEM((128, ROWS, HD), jnp.bfloat16),
            pltpu.VMEM((4, ROWS, GROUP * HD), jnp.bfloat16),
            pltpu.VMEM((GROUP // 2 * ROWS, WIN * ROWS), jnp.bfloat16),
            pltpu.VMEM((GROUP // 2 * ROWS, WIN * ROWS), jnp.bfloat16),
            pltpu.VMEM((WIN * ROWS, 2 * HD), jnp.bfloat16),
            pltpu.VMEM((WIN * ROWS, 2 * HD), jnp.bfloat16),
            pltpu.VMEM((8, ROWS), jnp.int32),
            pltpu.SMEM((8, ROWS), jnp.int32),
            pltpu.SMEM((ROWS,), jnp.int32),
            pltpu.SMEM((8,), jnp.int32),
            pltpu.VMEM((1, ROWS), jnp.int32),
            dma((3, 8)), dma((3, 8)),
            dma((80,)), dma((80,)),
            dma((4, 4, 2)), dma((4, 4, 2)),
            dma((13,)),
        ],
        compiler_params=pltpu.CompilerParams(
            collective_id=0, has_side_effects=True, vmem_limit_bytes=60 * 1024 * 1024),
    )(half_order, window, half_order.reshape(1, ROWS), queries, keys, values)


def solution(mesh):
    rows = P(("outer", "inner"), "head", None)
    return jax.shard_map(
        body,
        mesh=mesh,
        in_specs=(rows, rows, rows, P(), P()),
        out_specs=rows,
        check_vma=False,
    )
```

time: 81.4 us -> 76.9 us (0.945)
  local copies, waits for them, and re-layouts: 4.67 us -> 2.26 us
  Pallas kernels: 76.5 us -> 74.5 us
    unnamed x11 -> x1, local copies, waits for them, and re-layouts: 4.67 us -> 2.26 us
    pallas_call x1, Pallas kernels: 76.5 us -> 74.5 us  [body(): pl.pallas_call(kernel, out_shape=jax.ShapeDtypeStruct(queries.shape, jnp....]
where the time goes in v3:
time: 76.9 us; the launch traced here: 76.7 us
  Pallas kernels  74.5 us (97%)
  local copies, waits for them, and re-layouts  2.26 us (3%)
    pallas_call x1, Pallas kernels, body(): pl.pallas_call(kernel, out_shape=jax.ShapeDtypeStruct(queries.shape, jnp....  74.5 us
    unnamed x1, local copies, waits for them, and re-layouts  2.26 us

profile of v3, /device:TPU:1, one launch (start us, length us, event | category | flops | bytes accessed | tf_op | source)
XLA Modules:
  0.0 76.7 jit_solution(17229643234060630688)
XLA Ops:
  0.0 74.5 %shard_map.55 = bf16[2,32,8192]{2,1,0:T(8,128)(2,1)} custom-call(s32[128]{0:T(128)} %order_hbm.1, s32[8]{0:T(128)} %window_hbm.1, s32[1,128]{1,0:T(1,128)} %bitcast.1, bf16[2,32,8192]{2,1,0:T(8,128)(2,1)} %q_ref.1, bf16[2,32,1024]{2,1,0:T(8,128)(2,1)} %k_ref.1, bf16[2,32,1024]{2,1,0:T(8,128)(2,1)} %v_ref.1), custom_call_target="tpu_custom_call" | custom-call | tf_op jit(solution)/shard_map/pallas_call | solution.py:332
  74.5 2.3 %copy.7 = bf16[2,32,8192]{2,1,0:T(8,128)(2,1)} copy(bf16[2,32,8192]{2,1,0:T(8,128)(2,1)} %shard_map.55) | data formatting | bytes 2097152

commit v4 on v3

--- a/solution.py
+++ b/solution.py
@@ -14,7 +14,6 @@
 LOG2E = 1.4426950408889634
 TILE = 2
 VTILE = 2
-REL = [(dx, dzl) for dzl in (0, 1) for dx in range(4)]
 RING = (0, -1, 1, 2)
 MESH = pl.DeviceIdType.MESH
 
@@ -78,11 +77,11 @@
     zh = lax.axis_index("inner")
     y, zl, c = outer // 4, (outer // 2) % 2, outer % 2
 
-    def dev(dx=0, dy=0, dzl=0, dc=0, dzh=0):
+    def dev(dx=0, dy=0, dz=0, dc=0):
         yy = (y + dy + 4) % 4
-        ll = (zl + dzl) % 2
+        zz = (zh * 2 + zl + dz + 8) % 8
         cc = (c + dc) % 2
-        return {"head": (x + dx + 4) % 4, "outer": yy * 4 + ll * 2 + cc, "inner": (zh + dzh + 4) % 4}
+        return {"head": (x + dx + 4) % 4, "outer": yy * 4 + zz % 2 * 2 + cc, "inner": zz // 2}
 
     def slot(dy=0, dzh=0, dc=0):
         return ((((y + dy + 4) % 4) * 4 + (zh + dzh + 4) % 4) * 2 + (c + dc) % 2) * 4
@@ -92,8 +91,8 @@
     for copy in small:
         copy.start()
     barrier = pltpu.get_barrier_semaphore()
-    partners = [dev(dx=dx, dzl=dzl) for dx, dzl in REL[1:]]
-    partners += [dev(dzh=1), dev(dzh=-1), dev(dy=1), dev(dy=-1), dev(dc=1)]
+    partners = [dev(dx=dx, dz=dz) for dz in (0, 1, -1) for dx in range(4) if dx or dz]
+    partners += [dev(dz=2), dev(dz=-2), dev(dy=1), dev(dy=-1), dev(dc=1)]
     for partner in partners:
         pl.semaphore_signal(barrier, inc=1, device_id=partner, device_id_type=MESH)
     pl.semaphore_wait(barrier, len(partners))
@@ -102,22 +101,24 @@
 
     def exchange(src, width, dst, send, recv, here):
         arriving = []
-        for n, (dx, dzl) in enumerate(REL):
-            xx, ll = (x + dx) % 4, (zl + dzl) % 2
-            lanes = pl.ds(pl.multiple_of((xx * 2 + ll) * width, width), width)
+        for n, (dx, i) in enumerate((dx, i) for i in (None, 0, 1) for dx in range(4)):
+            other, dz = (0, 0) if i is None else (1, 1 - 2 * i)
+            take = slice(0, 2) if i is None else slice(i, i + 1)
+            item, count = (0, 2) if i is None else (2 + i, 1)
+            lanes = pl.ds(pl.multiple_of(((x + dx) % 4 * 2 + (zl + other) % 2) * width, width), width)
             if n == 0:
-                copy = pltpu.make_async_copy(src.at[:, :, lanes], dst(x, zl, dzl), here)
+                copy = pltpu.make_async_copy(src.at[take, :, lanes], dst(own, item, count, x), here)
                 copy.start()
                 arriving.append(copy.wait)
             else:
+                there_own = ((y * 4 + (zh * 2 + zl + dz + 8) % 8 // 2) * 2 + c) * 4
+                there = dict(device_id=dev(dx=dx, dz=dz), device_id_type=MESH)
                 copy = pltpu.make_async_remote_copy(
-                    src.at[:, :, lanes], dst(x, zl, dzl), send.at[n], recv.at[n],
-                    device_id=dev(dx=dx, dzl=dzl), device_id_type=MESH)
+                    src.at[take, :, lanes], dst(there_own, item, count, x), send.at[n], recv.at[n], **there)
                 copy.start()
                 sent.append(copy)
                 back = pltpu.make_async_remote_copy(
-                    src.at[:, :, lanes], dst((x - dx + 4) % 4, ll, dzl), send.at[n], recv.at[n],
-                    device_id=dev(dx=dx, dzl=dzl), device_id_type=MESH)
+                    src.at[take, :, lanes], dst(own, item, count, (x - dx + 4) % 4), send.at[n], recv.at[n], **there)
                 arriving.append(back.wait_recv)
         return arriving
 
@@ -127,26 +128,29 @@
     for which, src, buf in ((0, k_ref, kbuf), (1, v_ref, vbuf)):
         arriving += exchange(
             src, HD,
-            lambda xx, ll, dzl, buf=buf: buf.at[pl.ds(own + 2 * ll, 2), pl.ds(32 * xx, 32), :],
+            lambda base, item, count, xx, buf=buf: buf.at[pl.ds(base + item, count), pl.ds(32 * xx, 32), :],
             a_send.at[which], a_recv.at[which], local.at[which])
     for copy in small:
         copy.wait()
     lane = lax.broadcasted_iota(jnp.int32, (1, ROWS), 1)
     block = jnp.zeros((1, ROWS), jnp.int32)
     for b in range(4):
-        stored = ((y * 4 + (zl + b // 2) % 2 * 2 + c) * 4 + zh) * 2 + b % 2
+        zz = (zh * 2 + zl + (0, 0, 7, 1)[b]) % 8
+        stored = ((y * 4 + zz % 2 * 2 + c) * 4 + zz // 2) * 2 + b % 2
         block = jnp.where(lane // WIN == b, order_ref[stored], block)
     back = WIN - 1 - lane % WIN
     wanted = block - back
     j = lax.broadcasted_iota(jnp.int32, (ROWS, ROWS), 0)
-    slots = (((j // 32) * 4 + (j // 2) % 4) * 2 + (j // 8) % 2) * 4 + (j // 16) % 2 * 2 + j % 2
+    moved = (j // 16 + zl) % 2
+    zz = ((j // 2) % 4 * 2 + (j // 16) % 2 + moved * (1 - j % 2 * 2) + 8) % 8
+    slots = (((j // 32) * 4 + zz // 2) * 2 + (j // 8) % 2) * 4 + moved * 2 + j % 2
     order = jnp.broadcast_to(row_ref[...], (ROWS, ROWS)).T
     lookup[0:1, :] = jnp.sum(jnp.where(order == wanted, slots, 0), axis=0, keepdims=True)
     lookup[1:2, :] = ((wanted >= 0) & (back < window_ref[x * 2 + zl])).astype(jnp.int32)
     lookup[2:8, :] = jnp.zeros((6, ROWS), jnp.int32)
     listing = pltpu.make_async_copy(lookup, table, local.at[5])
     listing.start()
-    for wait in arriving[:8]:
+    for wait in arriving[:12]:
         wait()
 
     names = {}
@@ -174,13 +178,13 @@
         pending[w].append((name, w, slot(dy, dzh, 1) + off, count))
 
     def to_z(w):
-        send("z+", w, slot(), 4, dev(dzh=1))
-        send("z-", w, slot(), 4, dev(dzh=-1))
+        send("z+", w, slot(), 4, dev(dz=2))
+        send("z-", w, slot(), 4, dev(dz=-2))
 
     def from_z(w, r):
         arrived("z+" if r < 0 else "z-", w, slot(0, r), 4)
         half = 0 if r < 0 else 2
-        send(("zz", r), w, slot(0, r) + half, 2, dev(dzh=-r))
+        send(("zz", r), w, slot(0, r) + half, 2, dev(dz=-2 * r))
 
     def from_zz(w):
         arrived(("zz", -1), w, slot(0, 2), 2)
@@ -206,10 +210,19 @@
         arrived(("yy-", r), w, slot(2, r) + 2, 2)
         share(w, 2, r, 1)
 
+    def to_zy(w, r):
+        send(("zy", r), w, slot(r, r), 4, dev(dz=-2 * r))
+
+    def from_zy(w):
+        arrived(("zy", -1), w, slot(-1, 2), 4)
+        send(("yy+", 2), w, slot(-1, 2), 2, dev(dy=1))
+        arrived(("zy", 1), w, slot(1, 2), 4)
+        send(("yy-", 2), w, slot(1, 2) + 2, 2, dev(dy=-1))
+
     K, V = 0, 1
     to_z(K)
     to_y(K, 0)
-    for wait in arriving[8:]:
+    for wait in arriving[12:]:
         wait()
     to_z(V)
     to_y(V, 0)
@@ -229,29 +242,30 @@
     from_z(V, 1)
     to_y(V, 1)
     from_zz(K)
-    to_y(K, 2)
+    from_y(K, -1)
+    to_zy(K, -1)
+    from_y(K, 1)
+    to_zy(K, 1)
     queries_in = exchange(
         q_ref, GROUP * HD,
-        lambda xx, ll, dzl: qbuf.at[pl.ds(2 * dzl, 2), pl.ds(32 * xx, 32), :],
+        lambda base, item, count, xx: qbuf.at[pl.ds(item, count), pl.ds(32 * xx, 32), :],
         a_send.at[2], a_recv.at[2], local.at[2])
-    from_y(K, -1)
-    from_y(K, 1)
     share(K, 0, 2)
     share_y(K, -1)
     share_y(K, 1)
     from_zz(V)
     to_y(V, 2)
     opposite(K, 0)
-    from_y(K, 2)
+    from_zy(K)
     share_y(K, 2)
     for r in (-1, 1, 2):
         share(V, 0, r)
     share_y(V, 0)
     from_y(V, -1)
     from_y(V, 1)
+    from_y(V, 2)
     for r in (-1, 1, 2):
         opposite(K, r)
-    from_y(V, 2)
     share_y(V, -1)
     share_y(V, 1)
     opposite(V, 0)
@@ -267,21 +281,21 @@
     width = GROUP * HD // 2
 
     def returns(b, j, start):
-        dzl, i = b // 2, b % 2
+        other, i = b // 2, b % 2
         part = slice(j * width, (j + 1) * width)
 
         def copy_to(dx, xx, ll):
             lanes = pl.ds(pl.multiple_of((xx * 2 + ll) * 2 * width + j * width, width), width)
             return pltpu.make_async_remote_copy(
                 obuf.at[b, pl.ds(32 * ((x + dx) % 4), 32), part], o_ref.at[i, :, lanes],
-                o_send.at[b, dx, j], o_recv.at[b, dx, j], device_id=dev(dx=dx, dzl=dzl), device_id_type=MESH)
+                o_send.at[b, dx, j], o_recv.at[b, dx, j], device_id=dev(dx=dx, dz=other * (2 * b - 5)), device_id_type=MESH)
 
         def remote(dx):
             if start:
                 copy_to(dx, x, zl).start()
             else:
                 copy_to(dx, x, zl).wait_send()
-                copy_to(dx, (x - dx + 4) % 4, (zl + dzl) % 2).wait_recv()
+                copy_to(dx, (x - dx + 4) % 4, (zl + other) % 2).wait_recv()
 
         def here():
             lanes = pl.ds(pl.multiple_of((x * 2 + zl) * 2 * width + j * width, width), width)
@@ -291,8 +305,8 @@
 
         for dx in (2, 1, 3):
             remote(dx)
-        pl.when(dzl == 1)(lambda: remote(0))
-        pl.when(dzl == 0)(here)
+        pl.when(other == 1)(lambda: remote(0))
+        pl.when(other == 0)(here)
 
     def attend(n, last):
         b, after = (n + 2) % 4, (n + 3) % 4
@@ -348,7 +362,7 @@
             pltpu.SMEM((ROWS,), jnp.int32),
             pltpu.SMEM((8,), jnp.int32),
             pltpu.VMEM((1, ROWS), jnp.int32),
-            dma((3, 8)), dma((3, 8)),
+            dma((3, 12)), dma((3, 12)),
             dma((80,)), dma((80,)),
             dma((4, 4, 2)), dma((4, 4, 2)),
             dma((13,)),

time: 76.9 us -> 72.6 us (0.944)
  Pallas kernels: 74.5 us -> 70.2 us
    pallas_call x1, Pallas kernels: 74.5 us -> 70.2 us  [body(): pl.pallas_call(kernel, out_shape=jax.ShapeDtypeStruct(queries.shape, jnp....]
where the time goes in v4:
time: 72.6 us; the launch traced here: 72.4 us
  Pallas kernels  70.2 us (97%)
  local copies, waits for them, and re-layouts  2.26 us (3%)
    pallas_call x1, Pallas kernels, body(): pl.pallas_call(kernel, out_shape=jax.ShapeDtypeStruct(queries.shape, jnp....  70.2 us
    unnamed x1, local copies, waits for them, and re-layouts  2.26 us

profile of v4, /device:TPU:1, one launch (start us, length us, event | category | flops | bytes accessed | tf_op | source)
XLA Modules:
  0.0 72.4 jit_solution(6356582422072673271)
XLA Ops:
  0.0 70.2 %shard_map.55 = bf16[2,32,8192]{2,1,0:T(8,128)(2,1)} custom-call(s32[128]{0:T(128)} %order_hbm.1, s32[8]{0:T(128)} %window_hbm.1, s32[1,128]{1,0:T(1,128)} %bitcast.1, bf16[2,32,8192]{2,1,0:T(8,128)(2,1)} %q_ref.1, bf16[2,32,1024]{2,1,0:T(8,128)(2,1)} %k_ref.1, bf16[2,32,1024]{2,1,0:T(8,128)(2,1)} %v_ref.1), custom_call_target="tpu_custom_call" | custom-call | tf_op jit(solution)/shard_map/pallas_call | solution.py:346
  70.2 2.3 %copy.7 = bf16[2,32,8192]{2,1,0:T(8,128)(2,1)} copy(bf16[2,32,8192]{2,1,0:T(8,128)(2,1)} %shard_map.55) | data formatting | bytes 2097152

commit v5 on v4

--- a/solution.py
+++ b/solution.py
@@ -246,15 +246,15 @@
     to_zy(K, -1)
     from_y(K, 1)
     to_zy(K, 1)
-    queries_in = exchange(
-        q_ref, GROUP * HD,
-        lambda base, item, count, xx: qbuf.at[pl.ds(item, count), pl.ds(32 * xx, 32), :],
-        a_send.at[2], a_recv.at[2], local.at[2])
     share(K, 0, 2)
     share_y(K, -1)
     share_y(K, 1)
     from_zz(V)
     to_y(V, 2)
+    queries_in = exchange(
+        q_ref, GROUP * HD,
+        lambda base, item, count, xx: qbuf.at[pl.ds(item, count), pl.ds(32 * xx, 32), :],
+        a_send.at[2], a_recv.at[2], local.at[2])
     opposite(K, 0)
     from_zy(K)
     share_y(K, 2)
@@ -303,7 +303,7 @@
                 obuf.at[b, pl.ds(32 * x, 32), part], o_ref.at[i, :, lanes], local.at[9 + 2 * i + j])
             copy.start() if start else copy.wait()
 
-        for dx in (2, 1, 3):
+        for dx in (1, 3, 2):
             remote(dx)
         pl.when(other == 1)(lambda: remote(0))
         pl.when(other == 0)(here)
@@ -347,7 +347,7 @@
         kernel,
         out_shape=jax.ShapeDtypeStruct(queries.shape, jnp.bfloat16),
         in_specs=[hbm] * 6,
-        out_specs=hbm,
+        out_specs=pl.BlockSpec(memory_space=pl.ANY),
         scratch_shapes=[
             pltpu.VMEM((4, ROWS, GROUP * HD), jnp.bfloat16),
             pltpu.VMEM((128, ROWS, HD), jnp.bfloat16),
@@ -368,8 +368,9 @@
             dma((13,)),
         ],
         compiler_params=pltpu.CompilerParams(
-            collective_id=0, has_side_effects=True, vmem_limit_bytes=60 * 1024 * 1024),
-    )(half_order, window, half_order.reshape(1, ROWS), queries, keys, values)
+            collective_id=0, has_side_effects=True, vmem_limit_bytes=44 * 1024 * 1024),
+    )(*(pltpu.with_memory_space_constraint(v, pltpu.HBM) for v in (
+        half_order, window, half_order.reshape(1, ROWS), queries, keys, values)))
 
 
 def solution(mesh):

time: 72.6 us -> 70.9 us (0.977)
  local copies, waits for them, and re-layouts: 2.26 us -> 0.97 us
    unnamed x1, local copies, waits for them, and re-layouts: 2.26 us -> 0.97 us
where the time goes in v5:
time: 70.9 us; the launch traced here: 70.7 us
  Pallas kernels  69.8 us (98%)
  local copies, waits for them, and re-layouts  0.97 us (1%)
    pallas_call x1, Pallas kernels, body(): pl.pallas_call(kernel, out_shape=jax.ShapeDtypeStruct(queries.shape, jnp....  69.8 us

profile of v5, /device:TPU:1, one launch (start us, length us, event | category | flops | bytes accessed | tf_op | source)
XLA Modules:
  0.0 70.7 jit_solution(16772438471218377262)
XLA Ops:
  0.0 69.8 %shard_map.55 = bf16[2,32,8192]{2,1,0:T(8,128)(2,1)S(1)} custom-call(s32[128]{0:T(128)} %order_hbm.1, s32[8]{0:T(128)} %window_hbm.1, s32[1,128]{1,0:T(1,128)} %bitcast.1, bf16[2,32,8192]{2,1,0:T(8,128)(2,1)} %q_ref.1, bf16[2,32,1024]{2,1,0:T(8,128)(2,1)} %k_ref.1, bf16[2,32,1024]{2,1,0:T(8,128)(2,1)} %v_ref.1), custom_call_target="tpu_custom_call" | custom-call | tf_op jit(solution)/shard_map/pallas_call | solution.py:346
  69.8 1.0 %copy.7 = bf16[2,32,8192]{2,1,0:T(8,128)(2,1)} copy(bf16[2,32,8192]{2,1,0:T(8,128)(2,1)S(1)} %shard_map.55) | data formatting | bytes 2097152
